TPU v7x, 256 devices: a whole 4x4x8 slice. The times are simulated.
256 devices in a mesh: grp: 4 (over x), attn: 2 (over core), exp: 32 (over z, y).
Axes of the slice: x: 4, y: 4, z: 8, core: 2. Of those that a mesh axis runs over, the one named last changes fastest.
Arguments:
- hidden_rows: bfloat16 [32, 64, 5120], P('exp', 'grp', 'attn'), may hold values from -6 to 6
- routes: int32 [32, 64, 6], P('exp'), may hold values from 0 to 31, all different within a row; in each aligned block of 64 rows (0 to 63, 64 to 127, ..., all dimensions but the last counted through in order) at most 16 rows name the same one
- route_gain: float32 [32, 64, 6], P('exp'), may hold values from 0.1 to 1
- gate_weight: bfloat16 [32, 1536, 5120], P('exp', 'grp', 'attn'), may hold values from -0.078125 to 0.078125
- up_weight: bfloat16 [32, 1536, 5120], P('exp', 'grp', 'attn'), may hold values from -0.078125 to 0.078125
- down_weight: bfloat16 [32, 1536, 5120], P('exp', 'grp', 'attn'), may hold values from -0.21875 to 0.21875
Outputs:
- layer_out: bfloat16 [32, 64, 5120], P('exp', 'grp', 'attn')
Inputs may be any that keep to these rules, and one draw needn't show every extreme that they name: `routes`: each row names 6 different experts. Among the 64 rows of one line no expert is named more than 16 times, and in every draw some expert is named exactly 16 times by the rows of one line; every expert is named somewhere.
All inputs are finite; a program needn't handle non-finite values.
Results may differ from a plain program's by a relative error of at most 0.022.
Values may be sent and summed in bfloat16 or wider, within the bound.
A program may use at most 64 MiB of HBM per device.

v0:
```python
import jax
import jax.numpy as jnp
from jax import lax
from jax.sharding import PartitionSpec as P


def slot_tables(routes_line, experts, caps):
    slab = routes_line.shape[0]
    picks = (routes_line[:, :, None] == jnp.arange(experts, dtype=jnp.int32)[None, None, :]).astype(
        jnp.float32
    )
    counts = jnp.sum(picks, axis=1)
    lower = (jnp.arange(slab)[:, None] > jnp.arange(slab)[None, :]).astype(jnp.float32)
    before = jnp.dot(lower, counts, precision=lax.Precision.HIGHEST)
    grid = jnp.arange(caps).astype(jnp.float32)
    send = counts[:, :, None] * (before[:, :, None] == grid).astype(jnp.float32)
    send = jnp.transpose(send, (1, 2, 0)).reshape(experts * caps, slab)
    gather_tab = picks[:, :, :, None] * (before[:, None, :, None] == grid).astype(jnp.float32)
    gather_tab = gather_tab.reshape(slab, picks.shape[1], experts * caps)
    return (send.astype(jnp.bfloat16), gather_tab)


def body(hidden_rows, routes, route_gain, gate_weight, up_weight, down_weight):
    n_lines = lax.axis_size("exp")
    local_experts = gate_weight.shape[0]
    experts = n_lines * local_experts
    slab = routes.shape[1]
    topk = routes.shape[2]
    caps = min(slab, slab * topk * 4 // (3 * experts))
    send_tab, gather_tab = slot_tables(routes[0], experts, caps)
    block = hidden_rows[0]
    half_rows = block.shape[0]
    width = block.shape[1]
    whole = lax.all_gather(block, "grp", axis=0, tiled=True)
    outgoing = jnp.dot(send_tab, whole, preferred_element_type=jnp.float32).astype(jnp.bfloat16)
    outgoing = outgoing.reshape(n_lines, local_experts, caps, width)
    arrived = lax.all_to_all(outgoing, "exp", split_axis=0, concat_axis=0, tiled=True)
    gate = jnp.einsum("sjcd,jfd->sjcf", arrived, gate_weight, preferred_element_type=jnp.float32)
    upper = jnp.einsum("sjcd,jfd->sjcf", arrived, up_weight, preferred_element_type=jnp.float32)
    gate, upper = (
        lax.psum(gate.astype(jnp.bfloat16), "attn").astype(jnp.float32),
        lax.psum(upper.astype(jnp.bfloat16), "attn").astype(jnp.float32),
    )
    act = (jax.nn.silu(gate) * upper).astype(jnp.bfloat16)
    part = jnp.einsum(
        "sjcf,jfd->sjcd", act, down_weight, preferred_element_type=jnp.float32
    ).astype(jnp.bfloat16)
    summed = lax.psum(part, "grp").astype(jnp.float32)
    returned = lax.all_to_all(
        summed.astype(jnp.bfloat16), "exp", split_axis=0, concat_axis=0, tiled=True
    ).astype(summed.dtype)
    returned = returned.reshape(experts * caps, width)
    start = lax.axis_index("grp") * half_rows
    table = lax.dynamic_slice_in_dim(gather_tab, start, half_rows, 0)
    gains = lax.dynamic_slice_in_dim(route_gain[0], start, half_rows, 0)
    picked = jnp.einsum("skm,md->skd", table, returned, precision=lax.Precision.HIGHEST)
    moe = jnp.sum(gains[:, :, None] * picked, axis=1)
    return (block.astype(jnp.float32) + moe).astype(jnp.bfloat16)[None]


def solution(mesh):
    placed = (
        P("exp", "grp", "attn"),
        P("exp", None, None),
        P("exp", None, None),
        P("exp", "grp", "attn"),
        P("exp", "grp", "attn"),
        P("exp", "grp", "attn"),
    )
    return jax.shard_map(
        body, mesh=mesh, in_specs=placed, out_specs=P("exp", "grp", "attn"), check_vma=False
    )
```

profile of v0, /device:TPU:1, one launch (start us, length us, event | category | flops | bytes accessed | tf_op | source)
XLA Modules:
  0.0 282.2 jit_solution(11538392206814247062)
XLA Ops:
  6.5 0.0 copy-start
  6.5 0.0 all-reduce.6.cloned.1.call-start
  6.5 0.8 copy.25
  7.4 0.1 eq.73
  7.5 0.1 fusion.44
  7.6 11.6 %all-gather = bf16[1,64,2560]{2,1,0:T(8,128)(2,1)S(1)} all-gather(bf16[1,16,2560]{2,1,0:T(8,128)(2,1)} %param.6), channel_id=2, replica_groups=mesh['grp'=4,'attn'=2,'exp'=32] {'grp'}, dimensions={1}, use_global_device_ids=true | all-gather | bytes 409600 | tf_op jit(solution)/shard_map/all_gather | solution.py:34
  19.2 0.1 fusion.37
  19.3 0.8 convolution_convert_fusion.1
  20.1 0.0 copy-start.3
  20.1 69.4 %all_to_all.10 = bf16[32,1,16,2560]{3,2,1,0:T(8,128)(2,1)S(1)} all-to-all(bf16[32,1,16,2560]{3,2,1,0:T(8,128)(2,1)S(1)} %bitcast.92), channel_id=1, replica_groups=mesh['grp'=4,'attn'=2,'exp'=32] {'exp'}, dimensions={0} | all-to-all | bytes 5242880 | tf_op jit(solution)/shard_map/all_to_all | solution.py:37
  89.5 0.0 copy-done.3
  89.5 2.3 fusion.19
  91.8 0.0 copy-done.4
  91.8 2.3 fusion.24
  94.1 0.0 all-reduce.6.cloned.1.call-update
  94.1 0.0 all-reduce.4.cloned.1.call-start
  94.2 30.5 %all-reduce.6.cloned.1.call-done = (bf16[32,1,16,384]{3,2,0,1:T(8,128)(2,1)}, bf16[32,1,16,384]{3,2,0,1:T(8,128)(2,1)}) async-done(((bf16[32,1,16,384]{3,2,0,1:T(8,128)(2,1)}, bf16[32,1,16,384]{3,2,0,1:T(8,128)(2,1)}), (bf16[32,1,16,384]{3,2,0,1:T(8,128)(2,1)}, bf16[32,1,16,384]{3,2,0,1:T(8,128)(2,1)})) %all-reduce.6.cloned.1.call-update) | async-done | bytes 786448 | tf_op jit(solution)/shard_map/psum | solution.py:42
  124.7 0.0 copy-done
  124.7 4.2 %fusion = bf16[32,1,16,2560]{3,2,0,1:T(8,128)(2,1)} fusion(bf16[1,384,2560]{2,1,0:T(8,128)(2,1)S(1)} %copy-done, bf16[32,1,16,384]{3,2,0,1:T(8,128)(2,1)} %get-tuple-element.5, bf16[32,1,16,384]{3,2,0,1:T(8,128)(2,1)} %get-tuple-element.6), kind=kOutput, calls=%fused_computation.2 | convolution fusion | flops 1009516544 | bytes 5373952 | tf_op jit(solution)/shard_map/sjcf,jfd->sjcd/dot_general | solution.py:45
  128.8 0.0 all-reduce.4.cloned.1.call-update
  128.9 73.0 %all-reduce.4.cloned.1.call-done = bf16[32,1,16,2560]{3,2,0,1:T(8,128)(2,1)} async-done(((bf16[32,1,16,2560]{3,2,0,1:T(8,128)(2,1)}), bf16[32,1,16,2560]{3,2,0,1:T(8,128)(2,1)}) %all-reduce.4.cloned.1.call-update) | async-done | bytes 2621456 | tf_op jit(solution)/shard_map/psum | solution.py:48
  201.9 9.8 %all-to-all-start.1 = ((bf16[32,1,16,2560]{3,2,1,0:T(8,128)(2,1)}), bf16[32,1,16,2560]{3,2,1,0:T(8,128)(2,1)}, u32[]{:S(2)}, u32[]{:S(2)}) async-start(bf16[32,1,16,2560]{3,2,1,0:T(8,128)(2,1)} %bitcast.94), calls=%async_computation.1 | async-start | bytes 5242880 | tf_op jit(solution)/shard_map/all_to_all | solution.py:49
  211.8 0.1 fusion.38
  211.9 0.1 constant_dynamic-slice_fusion.2
  212.0 0.8 copy.15
  212.8 0.1 mul.51
  212.9 0.5 constant_dynamic-slice_fusion
  213.4 1.1 copy.21
  214.5 0.8 constant_dynamic-slice_fusion.1
  215.3 56.2 %all-to-all-done.1 = bf16[32,1,16,2560]{3,2,1,0:T(8,128)(2,1)} async-done(((bf16[32,1,16,2560]{3,2,1,0:T(8,128)(2,1)}), bf16[32,1,16,2560]{3,2,1,0:T(8,128)(2,1)}, u32[]{:S(2)}, u32[]{:S(2)}) %all-to-all-start.1) | async-done | bytes 2621472 | tf_op jit(solution)/shard_map/all_to_all | solution.py:49
  271.5 3.2 %fusion.18 = f32[16,2560]{1,0:T(8,128)S(1)} fusion(bf16[512,2560,1]{1,0,2:T(8,128)(2,1)} %bitcast.29, f32[16,6]{0,1:T(8,128)S(1)} %bitcast.99, f32[16,6,512]{2,0,1:T(8,128)} %copy.21, f32[16,512]{1,0:T(8,128)S(1)} %constant_dynamic-slice_fusion.1), kind=kOutput, calls=%fused_computation.13 | convolution fusion | flops 1510449152 | bytes 3015040 | tf_op jit(solution)/shard_map/skm,md->skd/dot_general | solution.py:56
  274.7 0.7 fusion.40
  (10 shorter events, 0.0 us)
Async XLA Ops:
  6.5 118.1 %copy-start = (bf16[1,384,2560]{2,1,0:T(8,128)(2,1)S(1)}, bf16[1,384,2560]{2,1,0:T(8,128)(2,1)}, u32[]{:S(2)}) copy-start(bf16[1,384,2560]{2,1,0:T(8,128)(2,1)} %param.11) | copy-start | bytes 5898244
  6.5 118.1 %all-reduce.6.cloned.1.call-start = ((), (), s32[]{:S(2)}) async-start(), calls=%async_computation.3 | async-start | bytes 1572864 | tf_op jit(solution)/shard_map/psum | solution.py:42
  20.1 69.4 %copy-start.3 = (bf16[1,384,2560]{2,1,0:T(8,128)(2,1)S(1)}, bf16[1,384,2560]{2,1,0:T(8,128)(2,1)}, u32[]{:S(2)}) copy-start(bf16[1,384,2560]{2,1,0:T(8,128)(2,1)} %param.10) | copy-start | bytes 5898244
  89.5 2.3 copy-start.4
  94.1 107.8 %all-reduce.4.cloned.1.call-start = ((), (), s32[]{:S(2)}) async-start(), calls=%async_computation.2 | async-start | bytes 5242880 | tf_op jit(solution)/shard_map/psum | solution.py:48
  201.9 10.0 %copy-start.2 = (f32[1,64,6]{1,0,2:T(1,128)S(1)}, f32[1,64,6]{1,0,2:T(1,128)}, u32[]{:S(2)}) copy-start(f32[1,64,6]{1,0,2:T(1,128)} %param.8) | copy-start | bytes 4612
  201.9 69.6 %all-to-all-start.1 = ((bf16[32,1,16,2560]{3,2,1,0:T(8,128)(2,1)}), bf16[32,1,16,2560]{3,2,1,0:T(8,128)(2,1)}, u32[]{:S(2)}, u32[]{:S(2)}) async-start(bf16[32,1,16,2560]{3,2,1,0:T(8,128)(2,1)} %bitcast.94), calls=%async_computation.1 | async-start | bytes 5242880 | tf_op jit(solution)/shard_map/all_to_all | solution.py:49
  214.5 60.2 %copy-start.1 = (bf16[1,16,2560]{2,1,0:T(8,128)(2,1)S(1)}, bf16[1,16,2560]{2,1,0:T(8,128)(2,1)}, u32[]{:S(2)}) copy-start(bf16[1,16,2560]{2,1,0:T(8,128)(2,1)} %param.6) | copy-start | bytes 245764
Sparse Core Ops, SparseCore 0:
  94.2 30.3 all-reduce.5
  129.0 72.8 all-reduce.3
where the time goes:
time: 283 us; the launch traced here: 282 us
  waiting for transfers between devices  160 us (57%)
  blocking collectives  80.9 us (29%)
  between operations  13.5 us (5%)
  matrix products  12.9 us (5%)
  starting transfers between devices  9.86 us (3%)
  local copies, waits for them, and re-layouts  4.28 us (2%)
    psum x1, waiting for transfers between devices, body(): summed = lax.psum(part, 'grp').astype(jnp.float32)  73 us
    all_to_all x1, blocking collectives, body(): lax.all_to_all(outgoing, 'exp', split_axis=0, concat_axis=0, tiled=True)  69.4 us
    all_to_all x1, waiting for transfers between devices, body(): lax.all_to_all(summed.astype(jnp.bfloat16), 'exp', split_axis=0, concat_a...  56.2 us
    psum x1, waiting for transfers between devices, body(): lax.psum(upper.astype(jnp.bfloat16), 'attn').astype(jnp.float32)  30.5 us
    all_gather x1, blocking collectives, body(): whole = lax.all_gather(block, 'grp', axis=0, tiled=True)  11.6 us
    all_to_all x1, starting transfers between devices, body(): lax.all_to_all(summed.astype(jnp.bfloat16), 'exp', split_axis=0, concat_a...  9.82 us
  transfers between devices with their start and end apart: 3, of which 3 were waited for; matrix products, arithmetic and copies ran while one was open for 1% of the time, Pallas kernels for 0%

commit v1 on v0

v1 whole, which is shorter than its diff:
```python
import functools

import jax
import jax.numpy as jnp
from jax import lax
from jax.experimental import pallas as pl
from jax.experimental.pallas import tpu as pltpu
from jax.sharding import PartitionSpec as P

MESH = pl.DeviceIdType.MESH
NT = (((1,), (1,)), ((), ()))
F32, BF16 = jnp.float32, jnp.bfloat16

REL = (0, 1, -1, 2, -2, 3, -3, 4)
AT = {r: i for i, r in enumerate(REL)}
SPAN = ((0, 1), (1, 2), (3, 2), (5, 2), (7, 1))
ZS, YS, GS, CAPS, SLAB = 8, 4, 4, 16, 64


def kernel(
    meta_ref, hid, wg, wu, wd, out,
    meta, rows, x_all, y_out, w_gu, w_d, sel, mix, gu, gu_out, gu_in, act,
    own, other, x_in, q_out, back, z_out, z_in, fin, fin_own, fin_in, result,
    sa, ra, sm, rm, sz, rz, sy, ry, sx, rx, sp, rp, sxb, rxb, syb, ryb, szb, rzb, sf, rf, sl,
):
    g, a, e = lax.axis_index("grp"), lax.axis_index("attn"), lax.axis_index("exp")
    z, y = e // YS, e % YS
    h = g % 2
    half = own.shape[-1]
    part = half // 2

    def at_x(d):
        return ((g + d + GS) % GS, a, e)

    def at_y(d):
        return (g, a, z * YS + (y + d + YS) % YS)

    def at_z(d):
        return (g, a, ((z + d + ZS) % ZS) * YS + y)

    core = (g, 1 - a, e)

    def cols(c, base=0):
        return pl.ds(base + c * part, part)

    started = []

    def send(src, dst, ss, rs, dev):
        copy = pltpu.make_async_remote_copy(
            src_ref=src, dst_ref=dst, send_sem=ss, recv_sem=rs, device_id=dev, device_id_type=MESH
        )
        copy.start()
        started.append(copy)
        return copy

    peers = [at_x(d) for d in (1, 2, 3)] + [at_y(d) for d in (1, 2, 3)]
    peers += [at_z(r) for r in REL[1:]] + [core]
    barrier = pltpu.get_barrier_semaphore()
    for dev in peers:
        pl.semaphore_signal(barrier, inc=1, device_id=dev, device_id_type=MESH)

    mine, theirs = h * half, (1 - h) * half
    local = []

    def load(src, dst):
        copy = pltpu.make_async_copy(src, dst, sl.at[len(local)])
        copy.start()
        local.append(copy)
        return copy

    my_rows = pl.ds(pl.multiple_of(g * 16, 16), 16)
    firsts = [
        load(hid.at[:, pl.ds(pl.multiple_of(mine + c * part, 128), part)], rows.at[c, 0, my_rows, :])
        for c in (0, 1)
    ]
    pl.semaphore_wait(barrier, len(peers))

    xa = {}
    for c in (0, 1):
        for d in (1, 3, 2):
            there = ((g + d) % 2) * half + c * part
            xa[c, d] = send(
                hid.at[:, pl.ds(pl.multiple_of(there, 128), part)],
                rows.at[c, 0, my_rows, :], sa.at[c, d - 1], ra.at[c, d - 1], at_x(d),
            )
    xm = {}
    for r in REL[1:]:
        back_at = AT[-r] if r != 4 else AT[4]
        xm[r] = send(meta_ref, meta.at[back_at], sm.at[AT[r] - 1], rm.at[AT[r] - 1], at_z(r))
    weights = []
    for src, dst in ((wg, w_gu.at[pl.ds(0, wg.shape[0])]), (wu, w_gu.at[pl.ds(wg.shape[0], wg.shape[0])]), (wd, w_d)):
        for at, start in ((0, mine), (half, theirs)):
            weights.append(load(src.at[:, pl.ds(pl.multiple_of(start, 128), half)], dst.at[:, pl.ds(at, half)]))
    meta[0] = meta_ref[...]

    slots = YS * CAPS
    slot = lax.broadcasted_iota(jnp.int32, (slots, 128), 0)
    expert = (z * YS + (y + slot // CAPS) % YS).astype(F32)
    place = (lax.broadcasted_iota(jnp.int32, (slots, SLAB), 0) % CAPS).astype(F32)
    r_in = lax.broadcasted_iota(jnp.int32, (SLAB, SLAB), 0)
    r_out = lax.broadcasted_iota(jnp.int32, (SLAB, SLAB), 1)
    earlier = (r_in < r_out).astype(F32).astype(BF16)
    eye = (r_in == r_out).astype(F32).astype(BF16)

    def table(i):
        block = meta[i]
        picks = jnp.zeros((slots, 128), F32)
        gains = jnp.zeros((slots, 128), F32)
        for k in range(6):
            hit = block[k : k + 1, :] == expert
            picks = jnp.where(hit, 1.0, picks)
            gains = gains + jnp.where(hit, block[8 + k : 9 + k, :], 0.0)
        picks, gains = picks[:, :SLAB], gains[:, :SLAB]
        before = jnp.dot(picks.astype(BF16), earlier, preferred_element_type=F32)
        here = jnp.where(before == place, picks, 0.0)
        sel[i] = here.astype(BF16)
        weighed = (here * gains).astype(BF16)
        mix[i] = lax.dot_general(eye, weighed, NT, preferred_element_type=F32).astype(BF16)

    zd, yd, xd, pd, xb, yb, zb, fb = {}, {}, {}, {}, {}, {}, {}, {}

    def z_send(s, c):
        for sign, k in ((1, 0), (-1, 1)):
            if s == 4 and c != k:
                continue
            src = AT[-sign * (s - 1)]
            dst = AT[-sign * s] if s < 4 else AT[4]
            zd[s, c, k] = send(rows.at[c, src], rows.at[c, dst], sz.at[c, k, s - 1], rz.at[c, k, s - 1], at_z(sign))

    def z_event(s, c):
        if s == 0:
            firsts[c].wait()
            for d in (1, 2, 3):
                xa[c, d].wait_recv()
        else:
            for k in (0, 1):
                if (s, c, k) in zd:
                    zd[s, c, k].wait_recv()
        if s < 4:
            z_send(s + 1, c)

    def select(s, c):
        i0, n = SPAN[s]
        for i in range(i0, i0 + n):
            got = jnp.dot(sel[i], rows[c, i], preferred_element_type=F32).astype(BF16)
            x_all[i, 0, :, cols(c)] = got[0:CAPS]
            for d in (1, 2, 3):
                y_out[i, d - 1, :, cols(c)] = got[d * CAPS : (d + 1) * CAPS]
        for d in (1, 3, 2):
            yd[s, c, d] = send(
                y_out.at[pl.ds(i0, n), d - 1, :, cols(c)], x_all.at[pl.ds(i0, n), YS - d, :, cols(c)],
                sy.at[c, s, d - 1], ry.at[c, s, d - 1], at_y(d),
            )

    def y_event(s, c):
        for d in (1, 3, 2):
            yd[s, c, d].wait_recv()
        i0, n = SPAN[s]
        for k, step in ((0, 1), (1, -1)):
            lines, blocks = (pl.ds(i0 + k, 1), pl.ds(0, YS)) if n == 2 else (pl.ds(i0, 1), pl.ds(2 * k, 2))
            xd[s, c, k] = send(
                x_all.at[lines, blocks, :, cols(c)], x_all.at[lines, blocks, :, cols(c, half)],
                sx.at[c, s, k], rx.at[c, s, k], at_x(step),
            )

    def x_event(s):
        for c in (0, 1):
            for k in (0, 1):
                xd[s, c, k].wait_recv()

    def project(i0, n, number):
        at = pl.ds(i0 * SLAB, n * SLAB)
        block = x_all[pl.ds(i0, n)].reshape(n * SLAB, 2 * half)
        made = lax.dot_general(block, w_gu[...], NT, preferred_element_type=F32)
        gu[at] = made
        gu_out[at] = made.astype(BF16)
        pd[number] = send(gu_out.at[at], gu_in.at[at], sp.at[number], rp.at[number], core)

    def activate(i0, n, number):
        pd[number].wait_recv()
        at = pl.ds(i0 * SLAB, n * SLAB)
        total = gu[at] + gu_in[at].astype(F32)
        ff = total.shape[1] // 2
        gate, up = total[:, :ff], total[:, ff:]
        act[at] = (gate / (1.0 + jnp.exp(-gate)) * up).astype(BF16)

    def down(s):
        i0, n = SPAN[s]
        block = act[pl.ds(i0 * SLAB, n * SLAB)]
        for c in (0, 1):
            made = jnp.dot(block, w_d[:, cols(c, half)], preferred_element_type=F32).astype(BF16)
            other[pl.ds(i0, n), :, :, cols(c)] = made.reshape(n, YS, CAPS, part)
            for k, step in ((0, 1), (1, -1)):
                lines, blocks = (pl.ds(i0 + k, 1), pl.ds(0, YS)) if n == 2 else (pl.ds(i0, 1), pl.ds(2 * k, 2))
                xb[s, c, k] = send(
                    other.at[lines, blocks, :, cols(c)], x_in.at[lines, blocks, :, cols(c)],
                    sxb.at[c, s, k], rxb.at[c, s, k], at_x(step),
                )
        for c in (0, 1):
            made = jnp.dot(block, w_d[:, cols(c)], preferred_element_type=F32)
            own[pl.ds(i0, n), :, :, cols(c)] = made.reshape(n, YS, CAPS, part)

    def xb_event(s, c):
        for k in (0, 1):
            xb[s, c, k].wait_recv()
        i0, n = SPAN[s]
        at = pl.ds(i0, n)
        total = (own[at, :, :, cols(c)] + x_in[at, :, :, cols(c)].astype(F32)).astype(BF16)
        back[at, 0, :, cols(c)] = total[:, 0]
        for d in (1, 2, 3):
            q_out[at, d - 1, :, cols(c)] = total[:, d]
        for d in (1, 3, 2):
            yb[s, c, d] = send(
                q_out.at[at, d - 1, :, cols(c)], back.at[at, YS - d, :, cols(c)],
                syb.at[c, s, d - 1], ryb.at[c, s, d - 1], at_y(d),
            )

    def yb_event(s, c):
        for d in (1, 3, 2):
            yb[s, c, d].wait_recv()
        i0, n = SPAN[s]
        if s == 0:
            total = jnp.dot(mix[0], back[0, :, :, cols(c)].reshape(slots, part), preferred_element_type=F32)
            for k in (0, 1):
                zb[1, c, k].wait_recv()
                total = total + z_in[c, k, 0].astype(F32)
            fin[c] = total.astype(BF16)
            for d in (1, 3, 2):
                to_rows = pl.ds(pl.multiple_of(((g + d) % GS) * 16, 16), 16)
                fb[c, d] = send(fin.at[c, to_rows], fin_in.at[c, d - 1], sf.at[c, d - 1], rf.at[c, d - 1], at_x(d))
            return
        for sign, k in ((1, 0), (-1, 1)):
            if s == 4 and c != k:
                continue
            i = AT[sign * s] if s < 4 else AT[4]
            total = jnp.dot(mix[i], back[i, :, :, cols(c)].reshape(slots, part), preferred_element_type=F32)
            if (s + 1, c, k) in zb:
                zb[s + 1, c, k].wait_recv()
                total = total + z_in[c, k, s].astype(F32)
            z_out[c, k, s - 1] = total.astype(BF16)
            zb[s, c, k] = send(
                z_out.at[c, k, s - 1], z_in.at[c, k, s - 1], szb.at[c, k, s - 1], rzb.at[c, k, s - 1], at_z(sign)
            )

    table(0)
    for c in (0, 1):
        z_event(0, c)
        select(0, c)
    for r in REL[1:]:
        xm[r].wait_recv()
    for i in range(1, ZS):
        table(i)
    z_event(1, 0)
    select(1, 0)
    y_event(0, 0)
    z_event(1, 1)
    select(1, 1)
    y_event(0, 1)
    z_event(2, 0)
    select(2, 0)
    y_event(1, 0)
    z_event(2, 1)
    select(2, 1)
    y_event(1, 1)
    for copy in weights:
        copy.wait()
    z_event(3, 0)
    select(3, 0)
    y_event(2, 0)
    z_event(3, 1)
    select(3, 1)
    y_event(2, 1)
    x_event(0)
    x_event(1)
    project(0, 3, 0)
    z_event(4, 0)
    select(4, 0)
    y_event(3, 0)
    z_event(4, 1)
    select(4, 1)
    y_event(3, 1)
    x_event(2)
    project(3, 2, 1)
    y_event(4, 0)
    y_event(4, 1)
    x_event(3)
    project(5, 2, 2)
    x_event(4)
    project(7, 1, 3)
    activate(5, 2, 2)
    down(3)
    activate(7, 1, 3)
    down(4)
    xb_event(3, 0)
    xb_event(3, 1)
    activate(3, 2, 1)
    down(2)
    xb_event(4, 0)
    xb_event(4, 1)
    activate(0, 3, 0)
    down(1)
    yb_event(4, 0)
    yb_event(4, 1)
    xb_event(2, 0)
    xb_event(2, 1)
    yb_event(3, 0)
    yb_event(3, 1)
    down(0)
    xb_event(1, 0)
    xb_event(1, 1)
    yb_event(2, 0)
    yb_event(2, 1)
    xb_event(0, 0)
    xb_event(0, 1)
    yb_event(1, 0)
    yb_event(1, 1)
    yb_event(0, 0)
    yb_event(0, 1)

    for c in (0, 1):
        for d in (1, 2, 3):
            fb[c, d].wait_recv()
        result[:, cols(c)] = fin[c, my_rows].astype(F32) + fin_in[c, 1].astype(F32)
        result[:, cols(c, half)] = fin_in[c, 0].astype(F32) + fin_in[c, 2].astype(F32)
    stores = []
    for at, start in ((0, mine), (half, theirs)):
        stores.append(load(result.at[:, pl.ds(at, half)], out.at[:, pl.ds(pl.multiple_of(start, 128), half)]))
    for copy in started:
        copy.wait_send()
    for copy in stores:
        copy.wait()


def body(hidden_rows, routes, route_gain, gate_weight, up_weight, down_weight):
    hid = hidden_rows[0]
    n, width = hid.shape
    ff = gate_weight.shape[1]
    half = width // 2
    part = half // 2
    picked = routes[0].astype(F32).T
    gains = route_gain[0].T
    pad = ((0, 2), (0, 128 - SLAB))
    meta = jnp.concatenate([jnp.pad(picked, pad, constant_values=-1.0), jnp.pad(gains, pad)], axis=0)
    total = ZS * SLAB
    vmem = pltpu.VMEM
    dma = pltpu.SemaphoreType.DMA
    pair = lambda *shape: [dma(shape), dma(shape)]
    any_spec = pl.BlockSpec(memory_space=pl.ANY)
    moe = pl.pallas_call(
        kernel,
        out_shape=jax.ShapeDtypeStruct((n, width), F32),
        in_specs=[pl.BlockSpec(memory_space=pltpu.VMEM)] + [any_spec] * 4,
        out_specs=any_spec,
        scratch_shapes=[
            vmem((ZS, 16, 128), F32),
            vmem((2, ZS, SLAB, part), BF16),
            vmem((ZS, YS, CAPS, width), BF16),
            vmem((ZS, 3, CAPS, half), BF16),
            vmem((2 * ff, width), BF16),
            vmem((ff, width), BF16),
            vmem((ZS, YS * CAPS, SLAB), BF16),
            vmem((ZS, SLAB, YS * CAPS), BF16),
            vmem((total, 2 * ff), F32),
            vmem((total, 2 * ff), BF16),
            vmem((total, 2 * ff), BF16),
            vmem((total, ff), BF16),
            vmem((ZS, YS, CAPS, half), F32),
            vmem((ZS, YS, CAPS, half), BF16),
            vmem((ZS, YS, CAPS, half), BF16),
            vmem((ZS, 3, CAPS, half), BF16),
            vmem((ZS, YS, CAPS, half), BF16),
            vmem((2, 2, 4, SLAB, part), BF16),
            vmem((2, 2, 4, SLAB, part), BF16),
            vmem((2, SLAB, part), BF16),
            vmem((2, 16, part), BF16),
            vmem((2, 3, 16, part), BF16),
            vmem((n, width), F32),
            *pair(2, 3), *pair(7), *pair(2, 2, 4), *pair(2, 5, 3), *pair(2, 5, 2), *pair(4),
            *pair(2, 5, 2), *pair(2, 5, 3), *pair(2, 2, 4), *pair(2, 3), dma((10,)),
        ],
        compiler_params=pltpu.CompilerParams(
            collective_id=0, has_side_effects=True, vmem_limit_bytes=60 * 1024 * 1024
        ),
        name="routed_layer",
    )(meta, hid, gate_weight[0], up_weight[0], down_weight[0])
    return (hid.astype(F32) + moe).astype(BF16)[None]


def solution(mesh):
    placed = (
        P("exp", "grp", "attn"),
        P("exp", None, None),
        P("exp", None, None),
        P("exp", "grp", "attn"),
        P("exp", "grp", "attn"),
        P("exp", "grp", "attn"),
    )
    return jax.shard_map(
        body, mesh=mesh, in_specs=placed, out_specs=P("exp", "grp", "attn"), check_vma=False
    )
```

time: 283 us -> 81.9 us (0.29)
  the two profiles are of different devices: /device:TPU:1 before, /device:TPU:2 now
where the time goes in v1:
time: 81.9 us; the launch traced here: 81.7 us
  Pallas kernels  78.1 us (95%)
  other arithmetic  2.86 us (3%)
    pallas_call x1, Pallas kernels, body(): pl.pallas_call(kernel, out_shape=jax.ShapeDtypeStruct((n, width), F32), i...  78.1 us

profile of v1, /device:TPU:2, one launch (start us, length us, event | category | flops | bytes accessed | tf_op | source)
XLA Modules:
  0.0 81.7 jit_solution(11345294800869504631)
XLA Ops:
  0.0 0.7 fusion.1
  0.7 0.7 copy.13
  1.4 0.6 select_maximum_fusion.meta_ref
  2.0 0.0 copy-start
  2.0 78.1 %routed_layer.1 = f32[16,2560]{1,0:T(8,128)} custom-call(f32[16,128]{1,0:T(8,128)} %select_maximum_fusion.meta_ref, bf16[16,2560]{1,0:T(8,128)(2,1)} %bitcast.19, bf16[384,2560]{1,0:T(8,128)(2,1)} %bitcast.16, bf16[384,2560]{1,0:T(8,128)(2,1)} %bitcast.17, bf16[384,2560]{1,0:T(8,128)(2,1)} %bitcast.18), custom_call_target="tpu_custom_call" | custom-call | tf_op jit(solution)/shard_map/routed_layer/pallas_call | solution.py:349
  80.1 0.0 copy-done
  80.1 1.6 %fusion = bf16[1,16,2560]{2,1,0:T(8,128)(2,1)} fusion(f32[16,2560]{1,0:T(8,128)} %routed_layer.1, bf16[1,16,2560]{2,1,0:T(8,128)(2,1)S(1)} %copy-done), kind=kLoop, calls=%fused_computation.1 | loop fusion | flops 122880 | bytes 327680 | tf_op jit(solution)/shard_map/broadcast_in_dim | solution.py:386
Async XLA Ops:
  2.0 78.1 %copy-start = (bf16[1,16,2560]{2,1,0:T(8,128)(2,1)S(1)}, bf16[1,16,2560]{2,1,0:T(8,128)(2,1)}, u32[]{:S(2)}) copy-start(bf16[1,16,2560]{2,1,0:T(8,128)(2,1)} %param.6) | copy-start | bytes 245764

commit v2 on v1

v2 whole, which is shorter than its diff:
```python
import functools

import jax
import jax.numpy as jnp
from jax import lax
from jax.experimental import pallas as pl
from jax.experimental.pallas import tpu as pltpu
from jax.sharding import PartitionSpec as P

MESH = pl.DeviceIdType.MESH
NT = (((1,), (1,)), ((), ()))
F32, BF16 = jnp.float32, jnp.bfloat16

REL = (0, 1, -1, 2, -2, 3, -3, 4)
AT = {r: i for i, r in enumerate(REL)}
SPAN = ((0, 1), (1, 2), (3, 2), (5, 2), (7, 1))
ZS, YS, GS, CAPS, SLAB = 8, 4, 4, 16, 64
PIECES = ((0, 5), (5, 5))
FAR = (0, 1)
CS = range(len(PIECES))
WAYS = ((1, 0), (-1, 1))

ORDER = (
    ("table", 0), ("z_event", 0, 0), ("select", 0, 0), ("z_event", 0, 1), ("select", 0, 1), ("tables",),
    ("z_event", 1, 0), ("select", 1, 0), ("y_event", 0, 0), ("y_event", 0, 1), ("z_event", 1, 1), ("select", 1, 1),
    ("z_event", 2, 0), ("select", 2, 0), ("y_event", 1, 0), ("z_event", 2, 1), ("select", 2, 1), ("y_event", 1, 1),
    ("z_event", 3, 0), ("select", 3, 0), ("y_event", 2, 0), ("z_event", 3, 1), ("select", 3, 1), ("y_event", 2, 1),
    ("loaded",), ("x_event", 0), ("x_event", 1), ("project", 0, 3, 0), ("z_event", 4, 0), ("select", 4, 0),
    ("z_event", 4, 1), ("select", 4, 1), ("y_event", 3, 0), ("y_event", 3, 1), ("x_event", 2),
    ("project", 3, 2, 1), ("y_event", 4, 0), ("y_event", 4, 1), ("activate", 0, 3, 0), ("x_event", 3),
    ("project", 5, 2, 2), ("x_event", 4), ("project", 7, 1, 3), ("activate", 5, 2, 2), ("activate", 7, 1, 3),
    ("down", 4), ("down", 3), ("activate", 3, 2, 1), ("down", 2), ("xb_event", 4, 0), ("xb_event", 4, 1),
    ("xb_event", 3, 0), ("xb_event", 3, 1), ("down", 1), ("yb_event", 4, 0), ("yb_event", 4, 1),
    ("xb_event", 2, 0), ("xb_event", 2, 1), ("down", 0), ("yb_event", 3, 0), ("yb_event", 3, 1),
    ("xb_event", 1, 0), ("xb_event", 1, 1), ("yb_event", 2, 0), ("yb_event", 2, 1), ("xb_event", 0, 0),
    ("xb_event", 0, 1), ("yb_event", 0, 0), ("yb_event", 0, 1), ("yb_event", 1, 0), ("yb_event", 1, 1),
    ("finish", 0), ("finish", 1),
)


def kernel(
    routes_ref, gains_ref, hid, wg, wu, wd, out,
    meta, rows, x_all, y_out, w_gu, w_d, sel, mix, gu, gu_out, gu_in, act,
    own, other, x_in, q_out, back, z_out, z_in, fin, fin_in, residual, result,
    sent, ra, rm, rz, ry, rx, rp, rxb, ryb, rzb, rf, sl,
):
    g, a, e = lax.axis_index("grp"), lax.axis_index("attn"), lax.axis_index("exp")
    z, y = e // YS, e % YS
    h = g % 2
    half = own.shape[-1]

    def at_x(d):
        return ((g + d + GS) % GS, a, e)

    def at_zx(sign, d):
        return ((g + d) % GS, a, ((z + sign + ZS) % ZS) * YS + y)

    def at_y(d):
        return (g, a, z * YS + (y + d + YS) % YS)

    def at_z(d):
        return (g, a, ((z + d + ZS) % ZS) * YS + y)

    core = (g, 1 - a, e)

    def cols(c, base=0):
        first, size = PIECES[c]
        return pl.ds(base + first * 128, size * 128)

    def send(src, dst, ss, rs, dev):
        pltpu.make_async_remote_copy(
            src_ref=src, dst_ref=dst, send_sem=sent.at[ss], recv_sem=rs, device_id=dev, device_id_type=MESH
        ).start()

    def await_all(ref, sem):
        pltpu.make_async_copy(ref, ref, sem).wait()

    peers = [at_x(d) for d in (1, 2, 3)] + [at_y(d) for d in (1, 2, 3)]
    peers += [at_z(r) for r in REL[1:]] + [core]
    peers += [at_zx(sign, d) for sign in (1, -1) for d in (1, 2, 3)]
    barrier = pltpu.get_barrier_semaphore()
    for dev in peers:
        pl.semaphore_signal(barrier, inc=1, device_id=dev, device_id_type=MESH)

    mine, theirs = h * half, (1 - h) * half
    def load(src, dst, sem):
        pltpu.make_async_copy(src, dst, sem).start()

    meta[0] = jnp.full(meta.shape[1:], -1.0, F32)
    for k in range(6):
        meta[0, k : k + 1, :SLAB] = routes_ref[k].astype(F32)
        meta[0, 8 + k : 9 + k, :SLAB] = gains_ref[k]

    my_rows = pl.ds(pl.multiple_of(g * 16, 16), 16)
    load(hid.at[:, pl.ds(pl.multiple_of(mine, 128), half)], rows.at[0, my_rows, :], sl.at[0])
    pl.semaphore_wait(barrier, len(peers))

    for c in CS:
        for sign, first in ((1, 3), (-1, 7), (0, -1)):
            for d in (1, 3, 2, 0) if sign else (1, 3, 2):
                there = ((g + d) % 2) * half + PIECES[c][0] * 128
                n = first + d
                send(
                    hid.at[:, pl.ds(pl.multiple_of(there, 128), PIECES[c][1] * 128)],
                    rows.at[AT[-sign], my_rows, cols(c)], 0, ra.at[c, abs(sign)], at_zx(sign, d),
                )
    for r in REL[1:]:
        back_at = AT[-r] if r != 4 else AT[4]
        send(meta.at[0], meta.at[back_at], 1, rm.at[0], at_z(r))
    for at, start in ((0, mine), (half, theirs)):
        there, here = pl.ds(pl.multiple_of(start, 128), half), pl.ds(at, half)
        load(wg.at[:, there], w_gu.at[pl.ds(0, wg.shape[0]), here], sl.at[1])
        load(wu.at[:, there], w_gu.at[pl.ds(wg.shape[0], wg.shape[0]), here], sl.at[1])
        load(wd.at[:, there], w_d.at[:, here], sl.at[2])
        load(hid.at[:, there], residual.at[:, here], sl.at[3])

    slots = YS * CAPS
    slot = lax.broadcasted_iota(jnp.int32, (slots, 128), 0)
    expert = (z * YS + (y + slot // CAPS) % YS).astype(F32)
    place = (lax.broadcasted_iota(jnp.int32, (slots, SLAB), 0) % CAPS).astype(F32)
    r_in = lax.broadcasted_iota(jnp.int32, (SLAB, SLAB), 0)
    r_out = lax.broadcasted_iota(jnp.int32, (SLAB, SLAB), 1)
    earlier = (r_in < r_out).astype(F32).astype(BF16)
    eye = (r_in == r_out).astype(F32).astype(BF16)

    def table(i):
        block = meta[i]
        picks = jnp.zeros((slots, 128), F32)
        gains = jnp.zeros((slots, 128), F32)
        for k in range(6):
            hit = block[k : k + 1, :] == expert
            picks = jnp.where(hit, 1.0, picks)
            gains = gains + jnp.where(hit, block[8 + k : 9 + k, :], 0.0)
        picks, gains = picks[:, :SLAB], gains[:, :SLAB]
        before = jnp.dot(picks.astype(BF16), earlier, preferred_element_type=F32)
        here = jnp.where(before == place, picks, 0.0)
        sel[i] = here.astype(BF16)
        weighed = (here * gains).astype(BF16)
        mix[i] = lax.dot_general(eye, weighed, NT, preferred_element_type=F32).astype(BF16)

    def z_send(s, c):
        for sign, k in WAYS:
            if s == 4 and FAR[c] != k:
                continue
            src = AT[-sign * (s - 1)]
            dst = AT[-sign * s] if s < 4 else AT[4]
            send(rows.at[src, :, cols(c)], rows.at[dst, :, cols(c)], 2, rz.at[c, s - 2], at_z(sign))

    def z_event(s, c):
        i0, n = SPAN[s]
        if s == 0:
            if c == 0:
                await_all(rows.at[0, my_rows, :], sl.at[0])
            await_all(rows.at[0, pl.ds(0, SLAB - 16), cols(c)], ra.at[c, 0])
        else:
            await_all(rows.at[pl.ds(i0, n), :, cols(c)], ra.at[c, 1] if s == 1 else rz.at[c, s - 2])
        if 1 <= s < 4:
            z_send(s + 1, c)

    def select(s, c):
        i0, n = SPAN[s]
        for i in range(i0, i0 + n):
            got = jnp.dot(sel[i], rows[i, :, cols(c)], preferred_element_type=F32).astype(BF16)
            x_all[i, 0, :, cols(c)] = got[0:CAPS]
            for d in (1, 2, 3):
                y_out[i, d - 1, :, cols(c)] = got[d * CAPS : (d + 1) * CAPS]
        for d in (1, 3, 2):
            send(
                y_out.at[pl.ds(i0, n), d - 1, :, cols(c)], x_all.at[pl.ds(i0, n), YS - d, :, cols(c)],
                3, ry.at[c, s], at_y(d),
            )

    def y_event(s, c):
        i0, n = SPAN[s]
        await_all(x_all.at[pl.ds(i0, n), pl.ds(1, 3), :, cols(c)], ry.at[c, s])
        for k, step in ((0, 1), (1, -1)):
            lines, blocks = (pl.ds(i0 + k, 1), pl.ds(0, YS)) if n == 2 else (pl.ds(i0, 1), pl.ds(2 * k, 2))
            send(
                x_all.at[lines, blocks, :, cols(c)], x_all.at[lines, blocks, :, cols(c, half)],
                4, rx.at[s], at_x(step),
            )

    def x_event(s):
        i0, n = SPAN[s]
        await_all(x_all.at[pl.ds(i0, n), :, :, pl.ds(half, half)], rx.at[s])

    def project(i0, n, number):
        at = pl.ds(i0 * SLAB, n * SLAB)
        block = x_all[pl.ds(i0, n)].reshape(n * SLAB, 2 * half)
        made = lax.dot_general(block, w_gu[...], NT, preferred_element_type=F32)
        gu[at] = made
        gu_out[at] = made.astype(BF16)
        send(gu_out.at[at], gu_in.at[at], 5, rp.at[number], core)

    def activate(i0, n, number):
        at = pl.ds(i0 * SLAB, n * SLAB)
        await_all(gu_in.at[at], rp.at[number])
        total = gu[at] + gu_in[at].astype(F32)
        ff = total.shape[1] // 2
        gate, up = total[:, :ff], total[:, ff:]
        act[at] = (gate / (1.0 + jnp.exp(-gate)) * up).astype(BF16)

    def down(s):
        i0, n = SPAN[s]
        block = act[pl.ds(i0 * SLAB, n * SLAB)]
        for c in CS:
            made = jnp.dot(block, w_d[:, cols(c, half)], preferred_element_type=F32).astype(BF16)
            other[pl.ds(i0, n), :, :, cols(c)] = made.reshape(n, YS, CAPS, made.shape[-1])
            for k, step in ((0, 1), (1, -1)):
                lines, blocks = (pl.ds(i0 + k, 1), pl.ds(0, YS)) if n == 2 else (pl.ds(i0, 1), pl.ds(2 * k, 2))
                send(
                    other.at[lines, blocks, :, cols(c)], x_in.at[lines, blocks, :, cols(c)],
                    6, rxb.at[c, s], at_x(step),
                )
        for c in CS:
            made = jnp.dot(block, w_d[:, cols(c)], preferred_element_type=F32)
            own[pl.ds(i0, n), :, :, cols(c)] = made.reshape(n, YS, CAPS, made.shape[-1])

    def xb_event(s, c):
        i0, n = SPAN[s]
        at = pl.ds(i0, n)
        await_all(x_in.at[at, :, :, cols(c)], rxb.at[c, s])
        total = (own[at, :, :, cols(c)] + x_in[at, :, :, cols(c)].astype(F32)).astype(BF16)
        back[at, 0, :, cols(c)] = total[:, 0]
        for d in (1, 2, 3):
            q_out[at, d - 1, :, cols(c)] = total[:, d]
        for d in (1, 3, 2):
            send(
                q_out.at[at, d - 1, :, cols(c)], back.at[at, YS - d, :, cols(c)],
                7, ryb.at[c, s], at_y(d),
            )

    def yb_event(s, c):
        i0, n = SPAN[s]
        await_all(back.at[pl.ds(i0, n), pl.ds(1, 3), :, cols(c)], ryb.at[c, s])
        width = PIECES[c][1] * 128
        if s == 0:
            total = jnp.dot(mix[0], back[0, :, :, cols(c)].reshape(slots, width), preferred_element_type=F32)
            fin[:, cols(c)] = total.astype(BF16)
            spread(fin, c, 0, -1, (1, 3, 2))
            return
        first_way = FAR[c] if s == 3 else 0
        for sign, k in WAYS:
            if s == 4 and FAR[c] != k:
                continue
            i = AT[sign * s] if s < 4 else AT[4]
            total = jnp.dot(mix[i], back[i, :, :, cols(c)].reshape(slots, width), preferred_element_type=F32)
            if s < 3 or (s == 3 and FAR[c] == k):
                if k == first_way:
                    ways = pl.ds(0, 2) if s < 3 else pl.ds(k, 1)
                    await_all(z_in.at[ways, s - 1, :, cols(c)], rzb.at[c, s - 1])
                total = total + z_in[k, s - 1, :, cols(c)].astype(F32)
            z_out[k, s - 1, :, cols(c)] = total.astype(BF16)
            if s == 1:
                spread(z_out.at[k, 0], c, sign, 3 + 4 * k, (1, 3, 2, 0))
            else:
                send(
                    z_out.at[k, s - 1, :, cols(c)], z_in.at[k, s - 2, :, cols(c)],
                    8, rzb.at[c, s - 2], at_z(sign),
                )

    def spread(src, c, sign, first, far):
        for d in far:
            to_rows = pl.ds(pl.multiple_of(((g + d) % GS) * 16, 16), 16)
            n = first + d
            send(src.at[to_rows, cols(c)], fin_in.at[n, :, cols(c)], 9, rf.at[c], at_zx(sign, d))

    def tables():
        await_all(meta.at[pl.ds(1, ZS - 1)], rm.at[0])
        for i in range(1, ZS):
            table(i)

    def loaded():
        for ref, n in ((w_gu, 1), (w_d, 2), (residual, 3)):
            await_all(ref, sl.at[n])

    def finish(c):
        await_all(fin_in.at[:, :, cols(c)], rf.at[c])
        here, there = cols(c), cols(c, half)
        moe = fin[my_rows, here].astype(F32)
        for n in (1, 3, 5, 7, 9):
            moe = moe + fin_in[n, :, here].astype(F32)
        result[:, here] = (residual[:, here].astype(F32) + moe).astype(BF16)
        moe = fin_in[0, :, here].astype(F32)
        for n in (2, 4, 6, 8, 10):
            moe = moe + fin_in[n, :, here].astype(F32)
        result[:, there] = (residual[:, there].astype(F32) + moe).astype(BF16)

    steps = dict(
        table=table, tables=tables, z_event=z_event, select=select, y_event=y_event, loaded=loaded, x_event=x_event,
        project=project, activate=activate, down=down, xb_event=xb_event, yb_event=yb_event, finish=finish,
    )
    for step, *given in ORDER:
        steps[step](*given)
    for at, start in ((0, mine), (half, theirs)):
        load(result.at[:, pl.ds(at, half)], out.at[:, pl.ds(pl.multiple_of(start, 128), half)], sl.at[4])
    five = rows.at[pl.ds(0, 5)]
    sizes = (fin_in, meta.at[pl.ds(0, ZS - 1)], five, y_out, other, gu_out, other, q_out, five, fin_in)
    for n, ref in enumerate(sizes):
        await_all(ref, sent.at[n])
    await_all(result, sl.at[4])


def body(hidden_rows, routes, route_gain, gate_weight, up_weight, down_weight):
    hid = hidden_rows[0]
    n, width = hid.shape
    ff = gate_weight.shape[1]
    half = width // 2
    picked, gains = (jnp.transpose(v, (2, 0, 1)) for v in (routes, route_gain))
    total, n_c = ZS * SLAB, len(PIECES)
    vmem = pltpu.VMEM
    dma = pltpu.SemaphoreType.DMA
    any_spec = pl.BlockSpec(memory_space=pl.ANY)
    out = pl.pallas_call(
        kernel,
        out_shape=jax.ShapeDtypeStruct((n, width), BF16),
        in_specs=[pl.BlockSpec(memory_space=pltpu.VMEM)] * 2 + [any_spec] * 4,
        out_specs=any_spec,
        scratch_shapes=[
            vmem((ZS, 16, 128), F32),
            vmem((ZS, SLAB, half), BF16),
            vmem((ZS, YS, CAPS, width), BF16),
            vmem((ZS, 3, CAPS, half), BF16),
            vmem((2 * ff, width), BF16),
            vmem((ff, width), BF16),
            vmem((ZS, YS * CAPS, SLAB), BF16),
            vmem((ZS, SLAB, YS * CAPS), BF16),
            vmem((total, 2 * ff), F32),
            vmem((total, 2 * ff), BF16),
            vmem((total, 2 * ff), BF16),
            vmem((total, ff), BF16),
            vmem((ZS, YS, CAPS, half), F32),
            vmem((ZS, YS, CAPS, half), BF16),
            vmem((ZS, YS, CAPS, half), BF16),
            vmem((ZS, 3, CAPS, half), BF16),
            vmem((ZS, YS, CAPS, half), BF16),
            vmem((2, 4, SLAB, half), BF16),
            vmem((2, 3, SLAB, half), BF16),
            vmem((SLAB, half), BF16),
            vmem((11, 16, half), BF16),
            vmem((n, width), BF16),
            vmem((n, width), BF16),
            dma((10,)), dma((n_c, 2)), dma((1,)), dma((n_c, 3)), dma((n_c, 5)), dma((5,)), dma((4,)),
            dma((n_c, 5)), dma((n_c, 5)), dma((n_c, 3)), dma((n_c,)), dma((5,)),
        ],
        compiler_params=pltpu.CompilerParams(
            collective_id=0, has_side_effects=True, vmem_limit_bytes=60 * 1024 * 1024
        ),
        name="routed_layer",
    )(picked, gains, hid, gate_weight[0], up_weight[0], down_weight[0])
    return out[None]


def solution(mesh):
    placed = (
        P("exp", "grp", "attn"),
        P("exp", None, None),
        P("exp", None, None),
        P("exp", "grp", "attn"),
        P("exp", "grp", "attn"),
        P("exp", "grp", "attn"),
    )
    return jax.shard_map(
        body, mesh=mesh, in_specs=placed, out_specs=P("exp", "grp", "attn"), check_vma=False
    )
```

time: 81.9 us -> 78.7 us (0.961)
  the two profiles are of different devices: /device:TPU:2 before, /device:TPU:1 now
where the time goes in v2:
time: 78.7 us; the launch traced here: 78.1 us
  Pallas kernels  76.5 us (97%)
  local copies, waits for them, and re-layouts  1.53 us (2%)
    pallas_call x1, Pallas kernels, body(): pl.pallas_call(kernel, out_shape=jax.ShapeDtypeStruct((n, width), BF16),...  76.5 us

profile of v2, /device:TPU:1, one launch (start us, length us, event | category | flops | bytes accessed | tf_op | source)
XLA Modules:
  0.0 78.1 jit_solution(17117820576563140165)
XLA Ops:
  0.0 76.5 %routed_layer.1 = bf16[16,2560]{1,0:T(8,128)(2,1)} custom-call(s32[6,1,64]{2,1,0:T(1,128)} %bitcast.12, f32[6,1,64]{2,1,0:T(1,128)} %bitcast.13, bf16[16,2560]{1,0:T(8,128)(2,1)} %bitcast.11, bf16[384,2560]{1,0:T(8,128)(2,1)} %bitcast.7, bf16[384,2560]{1,0:T(8,128)(2,1)} %bitcast.8, bf16[384,2560]{1,0:T(8,128)(2,1)} %bitcast.9), custom_call_target="tpu_custom_call" | custom-call | tf_op jit(solution)/shard_map/routed_layer/pallas_call | solution.py:314
  76.5 1.5 %copy.8 = bf16[1,16,2560]{2,1,0:T(8,128)(2,1)} copy(bf16[1,16,2560]{2,1,0:T(8,128)(2,1)} %bitcast.10) | data formatting | bytes 163840

commit v3 on v2

--- a/solution.py
+++ b/solution.py
@@ -15,33 +15,40 @@
 AT = {r: i for i, r in enumerate(REL)}
 SPAN = ((0, 1), (1, 2), (3, 2), (5, 2), (7, 1))
 ZS, YS, GS, CAPS, SLAB = 8, 4, 4, 16, 64
-PIECES = ((0, 5), (5, 5))
-FAR = (0, 1)
+PIECES = ((0, 3), (3, 2), (5, 3), (8, 2))
+FAR = (0, 1, 1, 0)
 CS = range(len(PIECES))
+PAIRS = ((0, 5), (5, 5))
 WAYS = ((1, 0), (-1, 1))
 
 ORDER = (
-    ("table", 0), ("z_event", 0, 0), ("select", 0, 0), ("z_event", 0, 1), ("select", 0, 1), ("tables",),
-    ("z_event", 1, 0), ("select", 1, 0), ("y_event", 0, 0), ("y_event", 0, 1), ("z_event", 1, 1), ("select", 1, 1),
-    ("z_event", 2, 0), ("select", 2, 0), ("y_event", 1, 0), ("z_event", 2, 1), ("select", 2, 1), ("y_event", 1, 1),
-    ("z_event", 3, 0), ("select", 3, 0), ("y_event", 2, 0), ("z_event", 3, 1), ("select", 3, 1), ("y_event", 2, 1),
-    ("loaded",), ("x_event", 0), ("x_event", 1), ("project", 0, 3, 0), ("z_event", 4, 0), ("select", 4, 0),
-    ("z_event", 4, 1), ("select", 4, 1), ("y_event", 3, 0), ("y_event", 3, 1), ("x_event", 2),
-    ("project", 3, 2, 1), ("y_event", 4, 0), ("y_event", 4, 1), ("activate", 0, 3, 0), ("x_event", 3),
-    ("project", 5, 2, 2), ("x_event", 4), ("project", 7, 1, 3), ("activate", 5, 2, 2), ("activate", 7, 1, 3),
-    ("down", 4), ("down", 3), ("activate", 3, 2, 1), ("down", 2), ("xb_event", 4, 0), ("xb_event", 4, 1),
-    ("xb_event", 3, 0), ("xb_event", 3, 1), ("down", 1), ("yb_event", 4, 0), ("yb_event", 4, 1),
-    ("xb_event", 2, 0), ("xb_event", 2, 1), ("down", 0), ("yb_event", 3, 0), ("yb_event", 3, 1),
-    ("xb_event", 1, 0), ("xb_event", 1, 1), ("yb_event", 2, 0), ("yb_event", 2, 1), ("xb_event", 0, 0),
-    ("xb_event", 0, 1), ("yb_event", 0, 0), ("yb_event", 0, 1), ("yb_event", 1, 0), ("yb_event", 1, 1),
-    ("finish", 0), ("finish", 1),
+    ("table", 0), ("z_event", 0, 0), ("z_event", 0, 1), ("z_event", 0, 2), ("z_event", 0, 3), ("select", 0, 0),
+    ("select", 0, 1), ("z_event", 1, 0), ("z_event", 1, 1), ("z_event", 1, 2), ("z_event", 1, 3), ("tables",),
+    ("table", 1), ("table", 2), ("select", 1, 0), ("select", 1, 1), ("table", 3), ("table", 4), ("z_event", 2, 0),
+    ("z_event", 2, 1), ("select", 2, 0), ("z_event", 2, 2), ("z_event", 2, 3), ("select", 2, 1), ("y_event", 0, 0),
+    ("y_event", 0, 1), ("y_event", 1, 0), ("y_event", 1, 1), ("table", 5), ("table", 6), ("z_event", 3, 0),
+    ("z_event", 3, 1), ("select", 3, 0), ("z_event", 3, 2), ("z_event", 3, 3), ("select", 3, 1), ("table", 7),
+    ("y_event", 2, 0), ("y_event", 2, 1), ("loaded",), ("project_own", 0, 3), ("z_event", 4, 0), ("z_event", 4, 1),
+    ("select", 4, 0), ("z_event", 4, 2), ("z_event", 4, 3), ("select", 4, 1), ("x_event", 0), ("x_event", 1),
+    ("project", 0, 3, 0), ("y_event", 3, 0), ("y_event", 3, 1), ("project_own", 3, 2), ("y_event", 4, 0),
+    ("y_event", 4, 1), ("x_event", 2), ("project", 3, 2, 1), ("project_own", 5, 2), ("project_own", 7, 1),
+    ("activate", 0, 3, 0), ("down", 1), ("activate", 3, 2, 1), ("weigh", 7), ("weigh", 5), ("weigh", 6),
+    ("weigh", 3), ("weigh", 4), ("weigh", 1), ("weigh", 2), ("weigh", 0), ("x_event", 3), ("project", 5, 2, 2),
+    ("x_event", 4), ("project", 7, 1, 3), ("activate", 5, 2, 2), ("activate", 7, 1, 3), ("down", 4), ("down", 3),
+    ("xb_event", 4, 0), ("xb_event", 4, 1), ("down", 2), ("xb_event", 3, 0), ("xb_event", 3, 1),
+    ("yb_event", 4, 0), ("yb_event", 4, 1), ("yb_event", 4, 2), ("yb_event", 4, 3), ("xb_event", 1, 0),
+    ("xb_event", 1, 1), ("down", 0), ("xb_event", 2, 0), ("xb_event", 2, 1), ("yb_event", 3, 0),
+    ("yb_event", 3, 1), ("yb_event", 3, 2), ("yb_event", 3, 3), ("xb_event", 0, 0), ("xb_event", 0, 1),
+    ("yb_event", 2, 0), ("yb_event", 2, 1), ("yb_event", 2, 2), ("yb_event", 2, 3), ("yb_event", 0, 0),
+    ("yb_event", 0, 1), ("yb_event", 0, 2), ("yb_event", 0, 3), ("yb_event", 1, 0), ("yb_event", 1, 1),
+    ("yb_event", 1, 2), ("yb_event", 1, 3), ("finish", 0), ("finish", 1), ("finish", 2), ("finish", 3),
 )
 
 
 def kernel(
     routes_ref, gains_ref, hid, wg, wu, wd, out,
     meta, rows, x_all, y_out, w_gu, w_d, sel, mix, gu, gu_out, gu_in, act,
-    own, other, x_in, q_out, back, z_out, z_in, fin, fin_in, residual, result,
+    own, other, x_in, q_out, back, z_out, z_in, fin, fin_in, residual,
     sent, ra, rm, rz, ry, rx, rp, rxb, ryb, rzb, rf, sl,
 ):
     g, a, e = lax.axis_index("grp"), lax.axis_index("attn"), lax.axis_index("exp")
@@ -65,6 +72,10 @@
 
     def cols(c, base=0):
         first, size = PIECES[c]
+        return pl.ds(base + first * 128, size * 128)
+
+    def pair(c, base=0):
+        first, size = PAIRS[c]
         return pl.ds(base + first * 128, size * 128)
 
     def send(src, dst, ss, rs, dev):
@@ -126,16 +137,18 @@
     def table(i):
         block = meta[i]
         picks = jnp.zeros((slots, 128), F32)
+        for k in range(6):
+            picks = jnp.where(block[k : k + 1, :] == expert, 1.0, picks)
+        picks = picks[:, :SLAB]
+        before = jnp.dot(picks.astype(BF16), earlier, preferred_element_type=F32)
+        sel[i] = jnp.where(before == place, picks, 0.0).astype(BF16)
+
+    def weigh(i):
+        block = meta[i]
         gains = jnp.zeros((slots, 128), F32)
         for k in range(6):
-            hit = block[k : k + 1, :] == expert
-            picks = jnp.where(hit, 1.0, picks)
-            gains = gains + jnp.where(hit, block[8 + k : 9 + k, :], 0.0)
-        picks, gains = picks[:, :SLAB], gains[:, :SLAB]
-        before = jnp.dot(picks.astype(BF16), earlier, preferred_element_type=F32)
-        here = jnp.where(before == place, picks, 0.0)
-        sel[i] = here.astype(BF16)
-        weighed = (here * gains).astype(BF16)
+            gains = jnp.where(block[k : k + 1, :] == expert, block[8 + k : 9 + k, :], gains)
+        weighed = (sel[i].astype(F32) * gains[:, :SLAB]).astype(BF16)
         mix[i] = lax.dot_general(eye, weighed, NT, preferred_element_type=F32).astype(BF16)
 
     def z_send(s, c):
@@ -160,23 +173,23 @@
     def select(s, c):
         i0, n = SPAN[s]
         for i in range(i0, i0 + n):
-            got = jnp.dot(sel[i], rows[i, :, cols(c)], preferred_element_type=F32).astype(BF16)
-            x_all[i, 0, :, cols(c)] = got[0:CAPS]
+            got = jnp.dot(sel[i], rows[i, :, pair(c)], preferred_element_type=F32).astype(BF16)
+            x_all[i, 0, :, pair(c)] = got[0:CAPS]
             for d in (1, 2, 3):
-                y_out[i, d - 1, :, cols(c)] = got[d * CAPS : (d + 1) * CAPS]
+                y_out[i, d - 1, :, pair(c)] = got[d * CAPS : (d + 1) * CAPS]
         for d in (1, 3, 2):
             send(
-                y_out.at[pl.ds(i0, n), d - 1, :, cols(c)], x_all.at[pl.ds(i0, n), YS - d, :, cols(c)],
+                y_out.at[pl.ds(i0, n), d - 1, :, pair(c)], x_all.at[pl.ds(i0, n), YS - d, :, pair(c)],
                 3, ry.at[c, s], at_y(d),
             )
 
     def y_event(s, c):
         i0, n = SPAN[s]
-        await_all(x_all.at[pl.ds(i0, n), pl.ds(1, 3), :, cols(c)], ry.at[c, s])
+        await_all(x_all.at[pl.ds(i0, n), pl.ds(1, 3), :, pair(c)], ry.at[c, s])
         for k, step in ((0, 1), (1, -1)):
             lines, blocks = (pl.ds(i0 + k, 1), pl.ds(0, YS)) if n == 2 else (pl.ds(i0, 1), pl.ds(2 * k, 2))
             send(
-                x_all.at[lines, blocks, :, cols(c)], x_all.at[lines, blocks, :, cols(c, half)],
+                x_all.at[lines, blocks, :, pair(c)], x_all.at[lines, blocks, :, pair(c, half)],
                 4, rx.at[s], at_x(step),
             )
 
@@ -184,10 +197,14 @@
         i0, n = SPAN[s]
         await_all(x_all.at[pl.ds(i0, n), :, :, pl.ds(half, half)], rx.at[s])
 
+    def project_own(i0, n):
+        block = x_all[pl.ds(i0, n), :, :, pl.ds(0, half)].reshape(n * SLAB, half)
+        gu[pl.ds(i0 * SLAB, n * SLAB)] = lax.dot_general(block, w_gu[:, :half], NT, preferred_element_type=F32)
+
     def project(i0, n, number):
         at = pl.ds(i0 * SLAB, n * SLAB)
-        block = x_all[pl.ds(i0, n)].reshape(n * SLAB, 2 * half)
-        made = lax.dot_general(block, w_gu[...], NT, preferred_element_type=F32)
+        block = x_all[pl.ds(i0, n), :, :, pl.ds(half, half)].reshape(n * SLAB, half)
+        made = gu[at] + lax.dot_general(block, w_gu[:, half:], NT, preferred_element_type=F32)
         gu[at] = made
         gu_out[at] = made.astype(BF16)
         send(gu_out.at[at], gu_in.at[at], 5, rp.at[number], core)
@@ -203,36 +220,37 @@
     def down(s):
         i0, n = SPAN[s]
         block = act[pl.ds(i0 * SLAB, n * SLAB)]
-        for c in CS:
-            made = jnp.dot(block, w_d[:, cols(c, half)], preferred_element_type=F32).astype(BF16)
-            other[pl.ds(i0, n), :, :, cols(c)] = made.reshape(n, YS, CAPS, made.shape[-1])
+        for c in (0, 1):
+            made = jnp.dot(block, w_d[:, pair(c, half)], preferred_element_type=F32).astype(BF16)
+            other[pl.ds(i0, n), :, :, pair(c)] = made.reshape(n, YS, CAPS, made.shape[-1])
             for k, step in ((0, 1), (1, -1)):
                 lines, blocks = (pl.ds(i0 + k, 1), pl.ds(0, YS)) if n == 2 else (pl.ds(i0, 1), pl.ds(2 * k, 2))
                 send(
-                    other.at[lines, blocks, :, cols(c)], x_in.at[lines, blocks, :, cols(c)],
+                    other.at[lines, blocks, :, pair(c)], x_in.at[lines, blocks, :, pair(c)],
                     6, rxb.at[c, s], at_x(step),
                 )
-        for c in CS:
-            made = jnp.dot(block, w_d[:, cols(c)], preferred_element_type=F32)
-            own[pl.ds(i0, n), :, :, cols(c)] = made.reshape(n, YS, CAPS, made.shape[-1])
+        for c in (0, 1):
+            made = jnp.dot(block, w_d[:, pair(c)], preferred_element_type=F32)
+            own[pl.ds(i0, n), :, :, pair(c)] = made.reshape(n, YS, CAPS, made.shape[-1])
 
     def xb_event(s, c):
         i0, n = SPAN[s]
         at = pl.ds(i0, n)
-        await_all(x_in.at[at, :, :, cols(c)], rxb.at[c, s])
-        total = (own[at, :, :, cols(c)] + x_in[at, :, :, cols(c)].astype(F32)).astype(BF16)
-        back[at, 0, :, cols(c)] = total[:, 0]
+        await_all(x_in.at[at, :, :, pair(c)], rxb.at[c, s])
+        total = (own[at, :, :, pair(c)] + x_in[at, :, :, pair(c)].astype(F32)).astype(BF16)
+        back[at, 0, :, pair(c)] = total[:, 0]
         for d in (1, 2, 3):
-            q_out[at, d - 1, :, cols(c)] = total[:, d]
+            q_out[at, d - 1, :, pair(c)] = total[:, d]
         for d in (1, 3, 2):
             send(
-                q_out.at[at, d - 1, :, cols(c)], back.at[at, YS - d, :, cols(c)],
+                q_out.at[at, d - 1, :, pair(c)], back.at[at, YS - d, :, pair(c)],
                 7, ryb.at[c, s], at_y(d),
             )
 
     def yb_event(s, c):
         i0, n = SPAN[s]
-        await_all(back.at[pl.ds(i0, n), pl.ds(1, 3), :, cols(c)], ryb.at[c, s])
+        if c % 2 == 0:
+            await_all(back.at[pl.ds(i0, n), pl.ds(1, 3), :, pair(c // 2)], ryb.at[c // 2, s])
         width = PIECES[c][1] * 128
         if s == 0:
             total = jnp.dot(mix[0], back[0, :, :, cols(c)].reshape(slots, width), preferred_element_type=F32)
@@ -267,8 +285,6 @@
 
     def tables():
         await_all(meta.at[pl.ds(1, ZS - 1)], rm.at[0])
-        for i in range(1, ZS):
-            table(i)
 
     def loaded():
         for ref, n in ((w_gu, 1), (w_d, 2), (residual, 3)):
@@ -280,25 +296,25 @@
         moe = fin[my_rows, here].astype(F32)
         for n in (1, 3, 5, 7, 9):
             moe = moe + fin_in[n, :, here].astype(F32)
-        result[:, here] = (residual[:, here].astype(F32) + moe).astype(BF16)
+        first, size = PIECES[c]
+        at = pl.ds(pl.multiple_of(mine + first * 128, 128), size * 128)
+        out[:, at] = (residual[:, here].astype(F32) + moe).astype(BF16)
         moe = fin_in[0, :, here].astype(F32)
         for n in (2, 4, 6, 8, 10):
             moe = moe + fin_in[n, :, here].astype(F32)
-        result[:, there] = (residual[:, there].astype(F32) + moe).astype(BF16)
+        at = pl.ds(pl.multiple_of(theirs + first * 128, 128), size * 128)
+        out[:, at] = (residual[:, there].astype(F32) + moe).astype(BF16)
 
     steps = dict(
-        table=table, tables=tables, z_event=z_event, select=select, y_event=y_event, loaded=loaded, x_event=x_event,
-        project=project, activate=activate, down=down, xb_event=xb_event, yb_event=yb_event, finish=finish,
+        table=table, tables=tables, weigh=weigh, z_event=z_event, select=select, y_event=y_event, loaded=loaded, x_event=x_event,
+        project_own=project_own, project=project, activate=activate, down=down, xb_event=xb_event, yb_event=yb_event, finish=finish,
     )
     for step, *given in ORDER:
         steps[step](*given)
-    for at, start in ((0, mine), (half, theirs)):
-        load(result.at[:, pl.ds(at, half)], out.at[:, pl.ds(pl.multiple_of(start, 128), half)], sl.at[4])
     five = rows.at[pl.ds(0, 5)]
     sizes = (fin_in, meta.at[pl.ds(0, ZS - 1)], five, y_out, other, gu_out, other, q_out, five, fin_in)
     for n, ref in enumerate(sizes):
         await_all(ref, sent.at[n])
-    await_all(result, sl.at[4])
 
 
 def body(hidden_rows, routes, route_gain, gate_weight, up_weight, down_weight):
@@ -313,9 +329,9 @@
     any_spec = pl.BlockSpec(memory_space=pl.ANY)
     out = pl.pallas_call(
         kernel,
-        out_shape=jax.ShapeDtypeStruct((n, width), BF16),
+        out_shape=pltpu.VMEM((n, width), BF16),
         in_specs=[pl.BlockSpec(memory_space=pltpu.VMEM)] * 2 + [any_spec] * 4,
-        out_specs=any_spec,
+        out_specs=pl.BlockSpec(memory_space=pltpu.VMEM),
         scratch_shapes=[
             vmem((ZS, 16, 128), F32),
             vmem((ZS, SLAB, half), BF16),
@@ -339,9 +355,8 @@
             vmem((SLAB, half), BF16),
             vmem((11, 16, half), BF16),
             vmem((n, width), BF16),
-            vmem((n, width), BF16),
-            dma((10,)), dma((n_c, 2)), dma((1,)), dma((n_c, 3)), dma((n_c, 5)), dma((5,)), dma((4,)),
-            dma((n_c, 5)), dma((n_c, 5)), dma((n_c, 3)), dma((n_c,)), dma((5,)),
+            dma((10,)), dma((n_c, 2)), dma((1,)), dma((n_c, 3)), dma((2, 5)), dma((5,)), dma((4,)),
+            dma((2, 5)), dma((2, 5)), dma((n_c, 3)), dma((n_c,)), dma((4,)),
         ],
         compiler_params=pltpu.CompilerParams(
             collective_id=0, has_side_effects=True, vmem_limit_bytes=60 * 1024 * 1024

time: 78.7 us -> 74.7 us (0.949)
  Pallas kernels: 76.5 us -> 74 us
  local copies, waits for them, and re-layouts: 1.53 us -> 0.64 us
    pallas_call x1, Pallas kernels: 76.5 us -> 74 us  [body(): pl.pallas_call(kernel, out_shape=pltpu.VMEM((n, width), BF16), in_specs=[...]
    unnamed x1, local copies, waits for them, and re-layouts: 1.53 us -> 0.64 us
where the time goes in v3:
time: 74.7 us; the launch traced here: 74.6 us
  Pallas kernels  74 us (99%)
    pallas_call x1, Pallas kernels, body(): pl.pallas_call(kernel, out_shape=pltpu.VMEM((n, width), BF16), in_specs=[...  74 us

profile of v3, /device:TPU:1, one launch (start us, length us, event | category | flops | bytes accessed | tf_op | source)
XLA Modules:
  0.0 74.6 jit_solution(13515957623574057498)
XLA Ops:
  0.0 74.0 %routed_layer.1 = bf16[16,2560]{1,0:T(8,128)(2,1)S(1)} custom-call(s32[6,1,64]{2,1,0:T(1,128)} %bitcast.12, f32[6,1,64]{2,1,0:T(1,128)} %bitcast.13, bf16[16,2560]{1,0:T(8,128)(2,1)} %bitcast.11, bf16[384,2560]{1,0:T(8,128)(2,1)} %bitcast.8, bf16[384,2560]{1,0:T(8,128)(2,1)} %bitcast.9, bf16[384,2560]{1,0:T(8,128)(2,1)} %bitcast.10), custom_call_target="tpu_custom_call" | custom-call | tf_op jit(solution)/shard_map/routed_layer/pallas_call | solution.py:330
  74.0 0.6 copy.8

commit v4 on v3

--- a/solution.py
+++ b/solution.py
@@ -22,26 +22,27 @@
 WAYS = ((1, 0), (-1, 1))
 
 ORDER = (
-    ("table", 0), ("z_event", 0, 0), ("z_event", 0, 1), ("z_event", 0, 2), ("z_event", 0, 3), ("select", 0, 0),
-    ("select", 0, 1), ("z_event", 1, 0), ("z_event", 1, 1), ("z_event", 1, 2), ("z_event", 1, 3), ("tables",),
-    ("table", 1), ("table", 2), ("select", 1, 0), ("select", 1, 1), ("table", 3), ("table", 4), ("z_event", 2, 0),
-    ("z_event", 2, 1), ("select", 2, 0), ("z_event", 2, 2), ("z_event", 2, 3), ("select", 2, 1), ("y_event", 0, 0),
-    ("y_event", 0, 1), ("y_event", 1, 0), ("y_event", 1, 1), ("table", 5), ("table", 6), ("z_event", 3, 0),
-    ("z_event", 3, 1), ("select", 3, 0), ("z_event", 3, 2), ("z_event", 3, 3), ("select", 3, 1), ("table", 7),
-    ("y_event", 2, 0), ("y_event", 2, 1), ("loaded",), ("project_own", 0, 3), ("z_event", 4, 0), ("z_event", 4, 1),
-    ("select", 4, 0), ("z_event", 4, 2), ("z_event", 4, 3), ("select", 4, 1), ("x_event", 0), ("x_event", 1),
-    ("project", 0, 3, 0), ("y_event", 3, 0), ("y_event", 3, 1), ("project_own", 3, 2), ("y_event", 4, 0),
-    ("y_event", 4, 1), ("x_event", 2), ("project", 3, 2, 1), ("project_own", 5, 2), ("project_own", 7, 1),
-    ("activate", 0, 3, 0), ("down", 1), ("activate", 3, 2, 1), ("weigh", 7), ("weigh", 5), ("weigh", 6),
-    ("weigh", 3), ("weigh", 4), ("weigh", 1), ("weigh", 2), ("weigh", 0), ("x_event", 3), ("project", 5, 2, 2),
-    ("x_event", 4), ("project", 7, 1, 3), ("activate", 5, 2, 2), ("activate", 7, 1, 3), ("down", 4), ("down", 3),
-    ("xb_event", 4, 0), ("xb_event", 4, 1), ("down", 2), ("xb_event", 3, 0), ("xb_event", 3, 1),
-    ("yb_event", 4, 0), ("yb_event", 4, 1), ("yb_event", 4, 2), ("yb_event", 4, 3), ("xb_event", 1, 0),
-    ("xb_event", 1, 1), ("down", 0), ("xb_event", 2, 0), ("xb_event", 2, 1), ("yb_event", 3, 0),
-    ("yb_event", 3, 1), ("yb_event", 3, 2), ("yb_event", 3, 3), ("xb_event", 0, 0), ("xb_event", 0, 1),
-    ("yb_event", 2, 0), ("yb_event", 2, 1), ("yb_event", 2, 2), ("yb_event", 2, 3), ("yb_event", 0, 0),
-    ("yb_event", 0, 1), ("yb_event", 0, 2), ("yb_event", 0, 3), ("yb_event", 1, 0), ("yb_event", 1, 1),
-    ("yb_event", 1, 2), ("yb_event", 1, 3), ("finish", 0), ("finish", 1), ("finish", 2), ("finish", 3),
+    ("table", 0), ("z_event", 0, 0), ("z_event", 0, 1), ("z_event", 0, 2), ("z_event", 0, 3), ("tables",),
+    ("table", 1), ("table", 2), ("z_event", 1, 0), ("z_event", 1, 1), ("z_event", 1, 2), ("z_event", 1, 3),
+    ("select", 0, 0), ("select", 0, 1), ("select", 1, 0), ("select", 1, 1), ("table", 3), ("table", 4),
+    ("z_event", 2, 0), ("z_event", 2, 1), ("select", 2, 0), ("z_event", 2, 2), ("z_event", 2, 3), ("select", 2, 1),
+    ("y_event", 0, 0), ("y_event", 0, 1), ("y_event", 1, 0), ("y_event", 1, 1), ("table", 5), ("table", 6),
+    ("z_event", 3, 0), ("z_event", 3, 1), ("select", 3, 0), ("z_event", 3, 2), ("z_event", 3, 3), ("select", 3, 1),
+    ("table", 7), ("y_event", 2, 0), ("y_event", 2, 1), ("loaded",), ("project_own", 0, 3), ("z_event", 4, 0),
+    ("z_event", 4, 1), ("select", 4, 0), ("z_event", 4, 2), ("z_event", 4, 3), ("select", 4, 1), ("x_event", 0),
+    ("x_event", 1), ("project", 0, 3, 0), ("y_event", 3, 0), ("y_event", 3, 1), ("project_own", 3, 2),
+    ("y_event", 4, 0), ("y_event", 4, 1), ("x_event", 2), ("project", 3, 2, 1), ("project_own", 5, 2),
+    ("project_own", 7, 1), ("activate", 0, 3, 0), ("activate", 3, 2, 1), ("down", 2), ("weigh", 7), ("weigh", 5),
+    ("weigh", 6), ("weigh", 3), ("weigh", 4), ("weigh", 1), ("weigh", 2), ("weigh", 0), ("x_event", 3),
+    ("project", 5, 2, 2), ("x_event", 4), ("project", 7, 1, 3), ("activate", 5, 2, 2), ("activate", 7, 1, 3),
+    ("down", 4), ("down", 3), ("down", 1), ("xb_event", 4, 0), ("xb_event", 4, 1), ("xb_event", 3, 0),
+    ("xb_event", 3, 1), ("yb_event", 4, 0), ("yb_event", 4, 1), ("yb_event", 4, 2), ("yb_event", 4, 3),
+    ("xb_event", 2, 0), ("xb_event", 2, 1), ("down", 0), ("xb_event", 1, 0), ("xb_event", 1, 1),
+    ("yb_event", 3, 0), ("yb_event", 3, 1), ("yb_event", 3, 2), ("yb_event", 3, 3), ("xb_event", 0, 0),
+    ("xb_event", 0, 1), ("yb_event", 2, 0), ("yb_event", 2, 1), ("yb_event", 2, 2), ("yb_event", 2, 3),
+    ("yb_event", 0, 0), ("yb_event", 0, 1), ("yb_event", 0, 2), ("yb_event", 0, 3), ("yb_event", 1, 0),
+    ("yb_event", 1, 1), ("yb_event", 1, 2), ("yb_event", 1, 3), ("finish", 0), ("finish", 1), ("finish", 2),
+    ("finish", 3),
 )
 
 

time: 74.7 us -> 72.1 us (0.965)
  Pallas kernels: 74 us -> 71.4 us
    pallas_call x1, Pallas kernels: 74 us -> 71.4 us  [body(): pl.pallas_call(kernel, out_shape=pltpu.VMEM((n, width), BF16), in_specs=[...]
where the time goes in v4:
time: 72.1 us; the launch traced here: 72 us
  Pallas kernels  71.4 us (99%)
    pallas_call x1, Pallas kernels, body(): pl.pallas_call(kernel, out_shape=pltpu.VMEM((n, width), BF16), in_specs=[...  71.4 us

profile of v4, /device:TPU:1, one launch (start us, length us, event | category | flops | bytes accessed | tf_op | source)
XLA Modules:
  0.0 72.0 jit_solution(1582791012564807461)
XLA Ops:
  0.0 71.4 %routed_layer.1 = bf16[16,2560]{1,0:T(8,128)(2,1)S(1)} custom-call(s32[6,1,64]{2,1,0:T(1,128)} %bitcast.12, f32[6,1,64]{2,1,0:T(1,128)} %bitcast.13, bf16[16,2560]{1,0:T(8,128)(2,1)} %bitcast.11, bf16[384,2560]{1,0:T(8,128)(2,1)} %bitcast.8, bf16[384,2560]{1,0:T(8,128)(2,1)} %bitcast.9, bf16[384,2560]{1,0:T(8,128)(2,1)} %bitcast.10), custom_call_target="tpu_custom_call" | custom-call | tf_op jit(solution)/shard_map/routed_layer/pallas_call | solution.py:331
  71.4 0.6 copy.8

commit v5 on v4

--- a/solution.py
+++ b/solution.py
@@ -33,16 +33,16 @@
     ("x_event", 1), ("project", 0, 3, 0), ("y_event", 3, 0), ("y_event", 3, 1), ("project_own", 3, 2),
     ("y_event", 4, 0), ("y_event", 4, 1), ("x_event", 2), ("project", 3, 2, 1), ("project_own", 5, 2),
     ("project_own", 7, 1), ("activate", 0, 3, 0), ("activate", 3, 2, 1), ("down", 2), ("weigh", 7), ("weigh", 5),
-    ("weigh", 6), ("weigh", 3), ("weigh", 4), ("weigh", 1), ("weigh", 2), ("weigh", 0), ("x_event", 3),
-    ("project", 5, 2, 2), ("x_event", 4), ("project", 7, 1, 3), ("activate", 5, 2, 2), ("activate", 7, 1, 3),
-    ("down", 4), ("down", 3), ("down", 1), ("xb_event", 4, 0), ("xb_event", 4, 1), ("xb_event", 3, 0),
-    ("xb_event", 3, 1), ("yb_event", 4, 0), ("yb_event", 4, 1), ("yb_event", 4, 2), ("yb_event", 4, 3),
-    ("xb_event", 2, 0), ("xb_event", 2, 1), ("down", 0), ("xb_event", 1, 0), ("xb_event", 1, 1),
-    ("yb_event", 3, 0), ("yb_event", 3, 1), ("yb_event", 3, 2), ("yb_event", 3, 3), ("xb_event", 0, 0),
-    ("xb_event", 0, 1), ("yb_event", 2, 0), ("yb_event", 2, 1), ("yb_event", 2, 2), ("yb_event", 2, 3),
-    ("yb_event", 0, 0), ("yb_event", 0, 1), ("yb_event", 0, 2), ("yb_event", 0, 3), ("yb_event", 1, 0),
-    ("yb_event", 1, 1), ("yb_event", 1, 2), ("yb_event", 1, 3), ("finish", 0), ("finish", 1), ("finish", 2),
-    ("finish", 3),
+    ("weigh", 6), ("weigh", 3), ("weigh", 4), ("weigh", 1), ("weigh", 2), ("weigh", 0), ("down_own", 2),
+    ("x_event", 3), ("project", 5, 2, 2), ("x_event", 4), ("project", 7, 1, 3), ("activate", 5, 2, 2),
+    ("activate", 7, 1, 3), ("down", 4), ("down", 3), ("down_own", 4), ("down_own", 3), ("down", 1),
+    ("xb_event", 4, 0), ("xb_event", 4, 1), ("xb_event", 3, 0), ("xb_event", 3, 1), ("yb_event", 4, 0),
+    ("yb_event", 4, 1), ("yb_event", 4, 2), ("yb_event", 4, 3), ("xb_event", 2, 0), ("xb_event", 2, 1),
+    ("down", 0), ("down_own", 1), ("xb_event", 1, 0), ("xb_event", 1, 1), ("yb_event", 3, 0), ("yb_event", 3, 1),
+    ("yb_event", 3, 2), ("yb_event", 3, 3), ("down_own", 0), ("xb_event", 0, 0), ("xb_event", 0, 1),
+    ("yb_event", 2, 0), ("yb_event", 2, 1), ("yb_event", 2, 2), ("yb_event", 2, 3), ("yb_event", 0, 0),
+    ("yb_event", 0, 1), ("yb_event", 0, 2), ("yb_event", 0, 3), ("yb_event", 1, 0), ("yb_event", 1, 1),
+    ("yb_event", 1, 2), ("yb_event", 1, 3), ("finish", 0), ("finish", 1), ("finish", 2), ("finish", 3),
 )
 
 
@@ -230,6 +230,10 @@
                     other.at[lines, blocks, :, pair(c)], x_in.at[lines, blocks, :, pair(c)],
                     6, rxb.at[c, s], at_x(step),
                 )
+
+    def down_own(s):
+        i0, n = SPAN[s]
+        block = act[pl.ds(i0 * SLAB, n * SLAB)]
         for c in (0, 1):
             made = jnp.dot(block, w_d[:, pair(c)], preferred_element_type=F32)
             own[pl.ds(i0, n), :, :, pair(c)] = made.reshape(n, YS, CAPS, made.shape[-1])
@@ -308,7 +312,7 @@
 
     steps = dict(
         table=table, tables=tables, weigh=weigh, z_event=z_event, select=select, y_event=y_event, loaded=loaded, x_event=x_event,
-        project_own=project_own, project=project, activate=activate, down=down, xb_event=xb_event, yb_event=yb_event, finish=finish,
+        project_own=project_own, project=project, activate=activate, down=down, down_own=down_own, xb_event=xb_event, yb_event=yb_event, finish=finish,
     )
     for step, *given in ORDER:
         steps[step](*given)

time: 72.1 us -> 72.2 us (level)
  no operation moved by 1% of the time
where the time goes in v5:
time: 72.2 us; the launch traced here: 72.1 us
  Pallas kernels  71.4 us (99%)
    pallas_call x1, Pallas kernels, body(): pl.pallas_call(kernel, out_shape=pltpu.VMEM((n, width), BF16), in_specs=[...  71.4 us

profile of v5, /device:TPU:1, one launch (start us, length us, event | category | flops | bytes accessed | tf_op | source)
XLA Modules:
  0.0 72.1 jit_solution(15399793846463102389)
XLA Ops:
  0.0 71.4 %routed_layer.1 = bf16[16,2560]{1,0:T(8,128)(2,1)S(1)} custom-call(s32[6,1,64]{2,1,0:T(1,128)} %bitcast.12, f32[6,1,64]{2,1,0:T(1,128)} %bitcast.13, bf16[16,2560]{1,0:T(8,128)(2,1)} %bitcast.11, bf16[384,2560]{1,0:T(8,128)(2,1)} %bitcast.8, bf16[384,2560]{1,0:T(8,128)(2,1)} %bitcast.9, bf16[384,2560]{1,0:T(8,128)(2,1)} %bitcast.10), custom_call_target="tpu_custom_call" | custom-call | tf_op jit(solution)/shard_map/routed_layer/pallas_call | solution.py:335
  71.4 0.6 copy.8

commit v6 on v5

--- a/solution.py
+++ b/solution.py
@@ -36,10 +36,12 @@
     ("weigh", 6), ("weigh", 3), ("weigh", 4), ("weigh", 1), ("weigh", 2), ("weigh", 0), ("down_own", 2),
     ("x_event", 3), ("project", 5, 2, 2), ("x_event", 4), ("project", 7, 1, 3), ("activate", 5, 2, 2),
     ("activate", 7, 1, 3), ("down", 4), ("down", 3), ("down_own", 4), ("down_own", 3), ("down", 1),
-    ("xb_event", 4, 0), ("xb_event", 4, 1), ("xb_event", 3, 0), ("xb_event", 3, 1), ("yb_event", 4, 0),
-    ("yb_event", 4, 1), ("yb_event", 4, 2), ("yb_event", 4, 3), ("xb_event", 2, 0), ("xb_event", 2, 1),
-    ("down", 0), ("down_own", 1), ("xb_event", 1, 0), ("xb_event", 1, 1), ("yb_event", 3, 0), ("yb_event", 3, 1),
-    ("yb_event", 3, 2), ("yb_event", 3, 3), ("down_own", 0), ("xb_event", 0, 0), ("xb_event", 0, 1),
+    ("xb_event", 4, 0), ("xb_event", 4, 1), ("xb_event", 4, 2), ("xb_event", 4, 3), ("xb_event", 3, 0),
+    ("xb_event", 3, 1), ("xb_event", 3, 2), ("xb_event", 3, 3), ("yb_event", 4, 0), ("yb_event", 4, 1),
+    ("yb_event", 4, 2), ("yb_event", 4, 3), ("xb_event", 2, 0), ("xb_event", 2, 1), ("xb_event", 2, 2),
+    ("xb_event", 2, 3), ("down", 0), ("down_own", 1), ("xb_event", 1, 0), ("xb_event", 1, 1), ("xb_event", 1, 2),
+    ("xb_event", 1, 3), ("yb_event", 3, 0), ("yb_event", 3, 1), ("yb_event", 3, 2), ("yb_event", 3, 3),
+    ("down_own", 0), ("xb_event", 0, 0), ("xb_event", 0, 1), ("xb_event", 0, 2), ("xb_event", 0, 3),
     ("yb_event", 2, 0), ("yb_event", 2, 1), ("yb_event", 2, 2), ("yb_event", 2, 3), ("yb_event", 0, 0),
     ("yb_event", 0, 1), ("yb_event", 0, 2), ("yb_event", 0, 3), ("yb_event", 1, 0), ("yb_event", 1, 1),
     ("yb_event", 1, 2), ("yb_event", 1, 3), ("finish", 0), ("finish", 1), ("finish", 2), ("finish", 3),
@@ -221,13 +223,13 @@
     def down(s):
         i0, n = SPAN[s]
         block = act[pl.ds(i0 * SLAB, n * SLAB)]
-        for c in (0, 1):
-            made = jnp.dot(block, w_d[:, pair(c, half)], preferred_element_type=F32).astype(BF16)
-            other[pl.ds(i0, n), :, :, pair(c)] = made.reshape(n, YS, CAPS, made.shape[-1])
+        for c in CS:
+            made = jnp.dot(block, w_d[:, cols(c, half)], preferred_element_type=F32).astype(BF16)
+            other[pl.ds(i0, n), :, :, cols(c)] = made.reshape(n, YS, CAPS, made.shape[-1])
             for k, step in ((0, 1), (1, -1)):
                 lines, blocks = (pl.ds(i0 + k, 1), pl.ds(0, YS)) if n == 2 else (pl.ds(i0, 1), pl.ds(2 * k, 2))
                 send(
-                    other.at[lines, blocks, :, pair(c)], x_in.at[lines, blocks, :, pair(c)],
+                    other.at[lines, blocks, :, cols(c)], x_in.at[lines, blocks, :, cols(c)],
                     6, rxb.at[c, s], at_x(step),
                 )
 
@@ -241,21 +243,20 @@
     def xb_event(s, c):
         i0, n = SPAN[s]
         at = pl.ds(i0, n)
-        await_all(x_in.at[at, :, :, pair(c)], rxb.at[c, s])
-        total = (own[at, :, :, pair(c)] + x_in[at, :, :, pair(c)].astype(F32)).astype(BF16)
-        back[at, 0, :, pair(c)] = total[:, 0]
+        await_all(x_in.at[at, :, :, cols(c)], rxb.at[c, s])
+        total = (own[at, :, :, cols(c)] + x_in[at, :, :, cols(c)].astype(F32)).astype(BF16)
+        back[at, 0, :, cols(c)] = total[:, 0]
         for d in (1, 2, 3):
-            q_out[at, d - 1, :, pair(c)] = total[:, d]
+            q_out[at, d - 1, :, cols(c)] = total[:, d]
         for d in (1, 3, 2):
             send(
-                q_out.at[at, d - 1, :, pair(c)], back.at[at, YS - d, :, pair(c)],
+                q_out.at[at, d - 1, :, cols(c)], back.at[at, YS - d, :, cols(c)],
                 7, ryb.at[c, s], at_y(d),
             )
 
     def yb_event(s, c):
         i0, n = SPAN[s]
-        if c % 2 == 0:
-            await_all(back.at[pl.ds(i0, n), pl.ds(1, 3), :, pair(c // 2)], ryb.at[c // 2, s])
+        await_all(back.at[pl.ds(i0, n), pl.ds(1, 3), :, cols(c)], ryb.at[c, s])
         width = PIECES[c][1] * 128
         if s == 0:
             total = jnp.dot(mix[0], back[0, :, :, cols(c)].reshape(slots, width), preferred_element_type=F32)
@@ -361,7 +362,7 @@
             vmem((11, 16, half), BF16),
             vmem((n, width), BF16),
             dma((10,)), dma((n_c, 2)), dma((1,)), dma((n_c, 3)), dma((2, 5)), dma((5,)), dma((4,)),
-            dma((2, 5)), dma((2, 5)), dma((n_c, 3)), dma((n_c,)), dma((4,)),
+            dma((n_c, 5)), dma((n_c, 5)), dma((n_c, 3)), dma((n_c,)), dma((4,)),
         ],
         compiler_params=pltpu.CompilerParams(
             collective_id=0, has_side_effects=True, vmem_limit_bytes=60 * 1024 * 1024

time: 72.2 us -> 72.1 us (level)
  no operation moved by 1% of the time
where the time goes in v6:
time: 72.1 us; the launch traced here: 72 us
  Pallas kernels  71.3 us (99%)
    pallas_call x1, Pallas kernels, body(): pl.pallas_call(kernel, out_shape=pltpu.VMEM((n, width), BF16), in_specs=[...  71.3 us

profile of v6, /device:TPU:1, one launch (start us, length us, event | category | flops | bytes accessed | tf_op | source)
XLA Modules:
  0.0 72.0 jit_solution(7710270129407769240)
XLA Ops:
  0.0 71.3 %routed_layer.1 = bf16[16,2560]{1,0:T(8,128)(2,1)S(1)} custom-call(s32[6,1,64]{2,1,0:T(1,128)} %bitcast.12, f32[6,1,64]{2,1,0:T(1,128)} %bitcast.13, bf16[16,2560]{1,0:T(8,128)(2,1)} %bitcast.11, bf16[384,2560]{1,0:T(8,128)(2,1)} %bitcast.8, bf16[384,2560]{1,0:T(8,128)(2,1)} %bitcast.9, bf16[384,2560]{1,0:T(8,128)(2,1)} %bitcast.10), custom_call_target="tpu_custom_call" | custom-call | tf_op jit(solution)/shard_map/routed_layer/pallas_call | solution.py:336
  71.4 0.6 copy.8
